TPU v7x, 512 devices: a whole 4x4x16 slice. The times are simulated.
512 devices in a mesh: expert: 64 (over y, x, z_hi, core), mp: 8 (over z_lo).
Axes of the slice: x: 4, y: 4, z: 16 (z_hi: 2, z_lo: 8; z = z_hi * 8 + z_lo), core: 2. Of those that a mesh axis runs over, the one named last changes fastest.
Arguments:
- tokens: bfloat16 [8192, 3584], P('expert'), may hold values from -6 to 6
- routes: int32 [8192, 2], P('expert'), may hold values from 0 to 31, all different within a row; in each aligned block of 128 rows (0 to 127, 128 to 255, ...) at most 16 rows name the same one
- gate_values: float32 [8192, 2], P('expert'), may hold values from 0.2 to 1
- expert_weights: bfloat16 [64, 3, 1792, 1024], P('expert', None, None, 'mp'), may hold values from -0.09375 to 0.09375
- old_owner: int32 [32], replicated, may hold values from 0 to 31, as said below
- new_owner: int32 [32], replicated, may hold values from 0 to 31, as said below
Outputs:
- mixed: bfloat16 [8192, 3584], P('expert', 'mp')
- relocated: bfloat16 [64, 3, 1792, 1024], P('expert', None, None, 'mp')
Inputs may be any that keep to these rules, and one draw needn't show every extreme that they name: `routes`: in each aligned block of 128 rows (the rows of one index of expert) no expert is named by more than 16 rows. `old_owner`: each slot holds exactly one expert. Each slot holds exactly one expert; exactly 2 experts have a new_owner other than their old_owner.
All inputs are finite; a program needn't handle non-finite values.
Results may differ from a plain program's by a relative error of at most 0.019.
Values may be sent and summed in bfloat16 or wider, within the bound.
No kernel may reach another device: no remote copies, remote signals or barrier semaphores. Data moves between devices by JAX's collectives and lax.ppermute only.
A program may use at most 64 MiB of HBM per device.

v0:
```python
import jax
import jax.numpy as jnp
from jax import lax
from jax.experimental.layout import Layout, with_layout_constraint
from jax.sharding import Mesh, PartitionSpec as P

PLANE = ("y", "x", "c")
NEAR = ("mb", "mc")
RING = ("zh", "ma", "mb", "mc")
CAP = 16


def swap(value, axis):
    return lax.ppermute(value, axis, [(0, 1), (1, 0)])


def mirrored(value):
    return lax.ppermute(value, RING, [(i, 15 - i) for i in range(16)])


def place_codes(routes, gate_values, owner):
    experts = owner.shape[0]
    flat = routes.T.reshape(-1)
    count = flat.shape[0]
    ids = jnp.arange(experts, dtype=jnp.int32)
    hot = (flat[:, None] == ids[None, :]).astype(jnp.bfloat16)
    at = jnp.arange(count, dtype=jnp.int32)
    earlier = (at[:, None] > at[None, :]).astype(jnp.bfloat16)
    before = jnp.dot(earlier, hot, preferred_element_type=jnp.float32)
    code = jnp.sum(
        hot.astype(jnp.float32) * (before + (owner * CAP).astype(jnp.float32)[None, :]), axis=1
    )
    return jnp.concatenate([code.reshape(routes.shape[1], -1), gate_values.T], axis=0)


def placed_rows(codes, zh):
    code = codes[:2].astype(jnp.int32)
    slot, rank = (code // CAP, code % CAP)
    row = jnp.where(slot % 2 == zh, slot // 2 * (2 * CAP) + rank, -2 * CAP)
    return jnp.stack([row, row + CAP], axis=1).reshape(2, -1)


def plane_rows():
    return 2 * CAP * lax.axis_size("y") * lax.axis_size("x")


def gather_rows(rows, table):
    at = jnp.arange(plane_rows(), dtype=jnp.int32)
    pick = ((rows[0][None, :] == at[:, None]) | (rows[1][None, :] == at[:, None])).astype(
        jnp.bfloat16
    )
    return jnp.dot(pick, table, preferred_element_type=jnp.float32).astype(jnp.bfloat16)


def exchange(rows, axes=PLANE):
    blocks = rows.reshape((lax.axis_size(axes), -1, rows.shape[-1]))
    return lax.all_to_all(blocks, axes, split_axis=0, concat_axis=0, tiled=True).reshape(rows.shape)


def expert_part(rows, weights):
    half = jnp.einsum("rd,gdf->grf", rows, weights[:2], preferred_element_type=jnp.float32)
    total = half + swap(half, "c")
    hidden = (jax.nn.silu(total[0]) * total[1]).astype(jnp.bfloat16)
    return lax.dot_general(
        hidden, weights[2], (((1,), (1,)), ((), ())), preferred_element_type=jnp.float32
    ).astype(jnp.bfloat16)


def weighted(back, codes, rows):
    at = jnp.arange(back.shape[0], dtype=jnp.int32)
    gate = jnp.concatenate([codes[2:4], codes[2:4]], axis=1)
    mix = sum((jnp.where(rows[k][:, None] == at[None, :], gate[k][:, None], 0.0) for k in range(2)))
    high = mix.astype(jnp.bfloat16)
    low = (mix - high.astype(jnp.float32)).astype(jnp.bfloat16)
    return jnp.dot(high, back, preferred_element_type=jnp.float32) + jnp.dot(
        low, back, preferred_element_type=jnp.float32
    )


def by_columns(mixed, near):
    tok_rows = mixed.shape[0] // 2
    parts = mixed.astype(jnp.bfloat16).reshape(2, tok_rows, 2, near, -1)
    return jnp.transpose(parts, (3, 2, 1, 0, 4)).reshape(near, 2, tok_rows, -1)


def near_sum(parts, place, mine, beside):
    count = parts.shape[0]
    own = lax.dynamic_index_in_dim(parts, place ^ mine, 0, keepdims=False)
    own, beside = tied((own, beside))
    total = own.astype(jnp.float32)
    for step in range(1, count):
        block = lax.dynamic_index_in_dim(parts, place ^ step ^ mine, 0, keepdims=False)
        total += lax.ppermute(block, NEAR, [(i, i ^ step) for i in range(count)]).astype(
            jnp.float32
        )
    return (total.astype(jnp.bfloat16), beside)


tied = lax.optimization_barrier


def pick_pieces(spread, old_owner, new_owner, zh):
    moved = new_owner != old_owner
    low = jnp.min(jnp.where(moved, old_owner, old_owner.shape[0]))
    high = jnp.max(jnp.where(moved, old_owner, -1))
    low_piece = lax.dynamic_index_in_dim(spread, low >> 1, 0, keepdims=False)
    high_piece = lax.dynamic_index_in_dim(spread, high >> 1, 0, keepdims=False)
    low_here, high_here = (low & 1 == zh, high & 1 == zh)
    other = swap(jnp.where(low_here, low_piece, high_piece), "zh")
    to_low = jnp.where(high_here, high_piece, other)
    to_high = jnp.where(low_here, low_piece, other)
    slots = 2 * jnp.arange(spread.shape[0], dtype=jnp.int32)[:, None, None] + zh
    return jnp.where(slots == low, to_low[None], jnp.where(slots == high, to_high[None], spread))


def shards(tokens, routes, gate_values, expert_weights, old_owner, new_owner):
    zh, far, place = (lax.axis_index("zh"), lax.axis_index("ma"), lax.axis_index(NEAR))
    near = lax.axis_size(NEAR)
    tok_rows = tokens.shape[0]
    own = expert_weights[0]
    table = jnp.transpose(tokens.reshape(tok_rows, 2 * near, 2, -1), (2, 0, 1, 3)).reshape(
        2 * tok_rows, -1
    )
    table = with_layout_constraint(table, Layout(major_to_minor=(0, 1)))
    share = 2 * tok_rows // near
    part = lax.dynamic_slice_in_dim(table, (near - 1 - place) * share, share, 0)
    codes = place_codes(routes, gate_values, old_owner)
    rows = placed_rows(codes, zh)
    quarter = mirrored(part)
    chips = lax.axis_size("y") * lax.axis_size("x")
    spread = lax.all_to_all(
        own.reshape(chips, -1, own.shape[-1]), ("y", "x"), split_axis=0, concat_axis=0, tiled=True
    )
    other_codes = mirrored(codes)
    payload, spread, quarter, other_codes = tied(
        (gather_rows(rows, table), spread, quarter, other_codes)
    )
    sent = exchange(payload)
    other_rows = placed_rows(other_codes, zh)
    other_table = lax.all_gather(quarter, NEAR, tiled=True)
    payload, sent = tied((gather_rows(other_rows, other_table), sent))
    other_sent = exchange(payload)
    chosen = pick_pieces(spread, old_owner, new_owner, zh)
    payload, other_sent, chosen = tied((expert_part(sent, own), other_sent, chosen))
    back = exchange(payload)
    payload, back = tied((expert_part(other_sent, own), back))
    other_back = exchange(payload)
    parts = by_columns(weighted(back, codes, rows), near)
    kept, other_back = near_sum(parts, place, 0, other_back)
    other_parts = by_columns(weighted(other_back, other_codes, other_rows), near)
    other_kept, chosen = near_sum(other_parts, place, near - 1, chosen)
    arrived = lax.all_to_all(chosen, ("y", "x"), split_axis=0, concat_axis=0, tiled=True)

    def of(value, index):
        return lax.dynamic_index_in_dim(value, index, 0, keepdims=False)

    total = of(kept, far).astype(jnp.float32)
    total += swap(of(kept, 1 - far), "ma").astype(jnp.float32)
    total += mirrored(of(other_kept, 1 - far)).astype(jnp.float32)
    total += lax.ppermute(of(other_kept, far), RING, [(i, i ^ 11) for i in range(16)]).astype(
        jnp.float32
    )
    return (total.astype(jnp.bfloat16), arrived.reshape(expert_weights.shape))


def solution(mesh):
    fine = Mesh(mesh.devices.reshape(4, 4, 2, 2, 2, 2, 2), ("y", "x", "zh", "c", "ma", "mb", "mc"))
    expert, mp = (("y", "x", "zh", "c"), ("ma", "mb", "mc"))
    in_specs = (
        P(expert, None),
        P(expert, None),
        P(expert, None),
        P(expert, None, None, mp),
        P(),
        P(),
    )
    out_specs = (P(expert, mp), P(expert, None, None, mp))
    return jax.shard_map(shards, mesh=fine, in_specs=in_specs, out_specs=out_specs, check_vma=False)
```

profile of v0, /device:TPU:99, one launch (start us, length us, event | category | flops | bytes accessed | tf_op | source)
XLA Modules:
  0.0 237.3 jit_solution(9027821609001539932)
XLA Ops:
  0.6 7.1 %all-to-all-start = ((bf16[16,336,128]{2,1,0:T(8,128)(2,1)}), bf16[16,336,128]{2,1,0:T(8,128)(2,1)S(1)}, u32[]{:S(2)}, u32[]{:S(2)}) async-start(bf16[16,336,128]{2,1,0:T(8,128)(2,1)} %bitcast.112), calls=%async_computation | async-start | bytes 2752512 | tf_op jit(solution)/shard_map/all_to_all | solution.py:131
  7.7 0.6 copy.9
  8.4 0.9 copy.16
  9.3 1.3 reshape.274
  10.6 11.1 %collective-permute-start = (bf16[64,1792]{1,0:T(8,128)(2,1)S(1)}, bf16[64,1792]{1,0:T(8,128)(2,1)S(1)}, u32[]{:S(2)}, u32[]{:S(2)}) collective-permute-start(bf16[64,1792]{1,0:T(8,128)(2,1)S(1)} %constant_dynamic-slice_fusion), channel_id=1, source_target_pairs={{0,23},{1,22},{2,21},{3,20},{4,19},{5,18},{6,17},{7,16},{16,7},{17... | collective-permute-start | bytes 688136 | tf_op jit(solution)/shard_map/ppermute | solution.py:18
  21.7 0.6 fusion.67
  22.4 0.2 fusion.13
  22.6 1.9 collective-permute-start.1
  24.6 1.9 convolution_convert_fusion.1
  26.5 7.1 %collective-permute-done.1 = f32[4,128]{1,0:T(4,128)S(1)} collective-permute-done((f32[4,128]{1,0:T(4,128)S(1)}, f32[4,128]{1,0:T(4,128)S(1)}, u32[]{:S(2)}, u32[]{:S(2)}) %collective-permute-start.1) | collective-permute-done | bytes 2080 | tf_op jit(solution)/shard_map/ppermute | solution.py:18
  33.6 9.8 %all-to-all-start.1 = ((bf16[32,16,1792]{2,1,0:T(8,128)(2,1)}), bf16[32,16,1792]{2,1,0:T(8,128)(2,1)S(1)}, u32[]{:S(2)}, u32[]{:S(2)}) async-start(bf16[32,16,1792]{2,1,0:T(8,128)(2,1)} %bitcast.16), calls=%async_computation.1 | async-start | bytes 3670016 | tf_op jit(solution)/shard_map/all_to_all | solution.py:57
  43.4 21.5 %all_gather.3 = bf16[256,1792]{1,0:T(8,128)(2,1)S(1)} all-gather(bf16[64,1792]{1,0:T(8,128)(2,1)S(1)} %collective-permute-done), channel_id=1, replica_groups=mesh['y'=4,'x'=4,'zh'=2,'c'=2,'ma'=2,'mb'=2,'mc'=2] {'mb','mc'}, dimensions={0}, use_global_device_ids=true | all-gather | bytes 1146880 | tf_op jit(solution)/shard_map/all_gather | solution.py:140
  65.0 1.9 convolution_convert_fusion
  66.9 0.9 all-to-all-done.1
  67.7 1.3 copy-done.3
  69.0 8.6 %all-to-all-start.2 = ((bf16[32,16,1792]{2,1,0:T(8,128)(2,1)}), bf16[32,16,1792]{2,1,0:T(8,128)(2,1)}, u32[]{:S(2)}, u32[]{:S(2)}) async-start(bf16[32,16,1792]{2,1,0:T(8,128)(2,1)} %bitcast.23), calls=%async_computation.2 | async-start | bytes 3670016 | tf_op jit(solution)/shard_map/all_to_all | solution.py:57
  80.2 1.3 fusion.69
  81.5 8.9 %collective-permute-start.3 = (bf16[336,128]{1,0:T(8,128)(2,1)S(1)}, bf16[336,128]{1,0:T(8,128)(2,1)S(1)}, u32[]{:S(2)}, u32[]{:S(2)}) collective-permute-start(bf16[336,128]{1,0:T(8,128)(2,1)S(1)} %bitcast_select_fusion.1), channel_id=1, source_target_pairs={{0,16},{16,0},{1,17},{17,1},{2,18},{18,2},{3,19},{19,3},{4,20},{20... | collective-permute-start | bytes 258056 | tf_op jit(solution)/shard_map/ppermute | solution.py:14
  90.4 2.1 fusion.6
  92.6 2.5 %collective-permute-start.2 = (f32[2,512,128]{2,1,0:T(8,128)S(1)}, f32[2,512,128]{2,1,0:T(8,128)S(1)}, u32[]{:S(2)}, u32[]{:S(2)}) collective-permute-start(f32[2,512,128]{2,1,0:T(8,128)S(1)} %fusion.6), channel_id=1, source_target_pairs={{0,8},{8,0},{1,9},{9,1},{2,10},{10,2},{3,11},{11,3},{4,12},{12,4},... | collective-permute-start | bytes 1572872 | tf_op jit(solution)/shard_map/ppermute | solution.py:14
  95.1 0.7 collective-permute-done.3
  95.9 1.3 select_select_fusion
  97.2 0.1 add.231
  97.3 1.9 convolution_convert_fusion.3
  99.2 2.8 %all-to-all-done.2 = bf16[32,16,1792]{2,1,0:T(8,128)(2,1)} async-done(((bf16[32,16,1792]{2,1,0:T(8,128)(2,1)}), bf16[32,16,1792]{2,1,0:T(8,128)(2,1)}, u32[]{:S(2)}, u32[]{:S(2)}) %all-to-all-start.2) | async-done | bytes 1835040 | tf_op jit(solution)/shard_map/all_to_all | solution.py:57
  102.0 7.5 %all-to-all-start.3 = ((bf16[32,16,1792]{2,1,0:T(8,128)(2,1)}), bf16[32,16,1792]{2,1,0:T(8,128)(2,1)S(1)}, u32[]{:S(2)}, u32[]{:S(2)}) async-start(bf16[32,16,1792]{2,1,0:T(8,128)(2,1)} %bitcast.110), calls=%async_computation.3 | async-start | bytes 3670016 | tf_op jit(solution)/shard_map/all_to_all | solution.py:57
  109.4 2.1 fusion.9
  111.6 2.3 collective-permute-start.4
  113.9 1.5 collective-permute-done.4
  115.4 0.1 add.237
  115.5 1.9 convolution_convert_fusion.2
  117.4 16.4 %all-to-all-done.3 = bf16[32,16,1792]{2,1,0:T(8,128)(2,1)S(1)} async-done(((bf16[32,16,1792]{2,1,0:T(8,128)(2,1)}), bf16[32,16,1792]{2,1,0:T(8,128)(2,1)S(1)}, u32[]{:S(2)}, u32[]{:S(2)}) %all-to-all-start.3) | async-done | bytes 1835040 | tf_op jit(solution)/shard_map/all_to_all | solution.py:57
  133.8 1.2 copy-done
  135.0 6.5 %all-to-all-start.4 = ((bf16[32,16,1792]{2,1,0:T(8,128)(2,1)}), bf16[32,16,1792]{2,1,0:T(8,128)(2,1)S(1)}, u32[]{:S(2)}, u32[]{:S(2)}) async-start(bf16[32,16,1792]{2,1,0:T(8,128)(2,1)} %bitcast.109), calls=%async_computation.4 | async-start | bytes 3670016 | tf_op jit(solution)/shard_map/all_to_all | solution.py:57
  141.6 2.4 fusion.45
  144.0 1.7 fusion
  145.7 3.5 %reshape.275 = bf16[2,128,2,4,224]{4,3,2,1,0:T(4,128)(2,1)S(1)} reshape(bf16[256,1792]{1,0:T(8,128)(2,1)} %fusion) | data formatting | bytes 1835008 | tf_op jit(solution)/shard_map/reshape | solution.py:82
  149.2 2.3 copy.18
  151.5 1.3 copy.13
  152.8 0.8 dynamic-slice_bitcast_fusion.6
  153.5 1.9 collective-permute-start.5
  155.5 10.1 %collective-permute-start.6 = (bf16[2,128,448]{1,2,0:T(8,128)(2,1)S(1)}, bf16[2,128,448]{1,2,0:T(8,128)(2,1)}, u32[]{:S(2)}, u32[]{:S(2)}) collective-permute-start(bf16[2,128,448]{1,2,0:T(8,128)(2,1)S(1)} %get-tuple-element.42), channel_id=1, source_target_pairs={{0,2},{1,3},{2,0},{3,1},{4,6},{5,7},{6,4},{7,5},{8,10},{9,11},{10,... | collective-permute-start | bytes 688136 | tf_op jit(solution)/shard_map/ppermute | solution.py:93
  165.5 1.9 collective-permute-start.7
  167.5 0.7 fusion.48
  168.2 0.8 fusion.1
  169.0 1.5 reshape.276
  170.5 1.4 copy.19
  171.9 0.1 copy.15
  172.0 0.1 dynamic-slice_bitcast_fusion.3
  172.1 6.8 %all-to-all-start.5 = ((bf16[16,336,128]{2,1,0:T(8,128)(2,1)}), bf16[16,336,128]{2,1,0:T(8,128)(2,1)S(1)}, u32[]{:S(2)}, u32[]{:S(2)}) async-start(bf16[16,336,128]{2,1,0:T(8,128)(2,1)} %select_select_fusion), calls=%async_computation.5 | async-start | bytes 2752512 | tf_op jit(solution)/shard_map/all_to_all | solution.py:152
  178.9 3.1 %collective-permute-start.10 = (bf16[2,128,448]{1,2,0:T(8,128)(2,1)S(1)}, bf16[2,128,448]{1,2,0:T(8,128)(2,1)S(1)}, u32[]{:S(2)}, u32[]{:S(2)}) collective-permute-start(bf16[2,128,448]{1,2,0:T(8,128)(2,1)S(1)} %get-tuple-element.46), channel_id=1, source_target_pairs={{0,2},{1,3},{2,0},{3,1},{4,6},{5,7},{6,4},{7,5},{8,10},{9,11},{10,... | collective-permute-start | bytes 688136 | tf_op jit(solution)/shard_map/ppermute | solution.py:93
  182.0 5.3 %collective-permute-start.11 = (bf16[2,128,448]{1,2,0:T(8,128)(2,1)S(1)}, bf16[2,128,448]{1,2,0:T(8,128)(2,1)S(1)}, u32[]{:S(2)}, u32[]{:S(2)}) collective-permute-start(bf16[2,128,448]{1,2,0:T(8,128)(2,1)S(1)} %get-tuple-element.45), channel_id=1, source_target_pairs={{0,3},{1,2},{2,1},{3,0},{4,7},{5,6},{6,5},{7,4},{8,11},{9,10},{10,... | collective-permute-start | bytes 688136 | tf_op jit(solution)/shard_map/ppermute | solution.py:93
  187.3 2.2 collective-permute-start.9
  189.5 1.3 add_convert_fusion.1
  190.8 5.9 %collective-permute-start.8 = (bf16[128,448]{0,1:T(8,128)(2,1)S(1)}, bf16[128,448]{0,1:T(8,128)(2,1)S(1)}, u32[]{:S(2)}, u32[]{:S(2)}) collective-permute-start(bf16[128,448]{0,1:T(8,128)(2,1)S(1)} %dynamic-slice_bitcast_fusion.10), channel_id=1, source_target_pairs={{0,4},{4,0},{1,5},{5,1},{2,6},{6,2},{3,7},{7,3},{8,12},{12,8},{9,1... | collective-permute-start | bytes 344072 | tf_op jit(solution)/shard_map/ppermute | solution.py:14
  196.8 4.6 %collective-permute-done.10 = bf16[2,128,448]{1,2,0:T(8,128)(2,1)S(1)} collective-permute-done((bf16[2,128,448]{1,2,0:T(8,128)(2,1)S(1)}, bf16[2,128,448]{1,2,0:T(8,128)(2,1)S(1)}, u32[]{:S(2)}, u32[]{:S(2)}) %collective-permute-start.10) | collective-permute-done | bytes 229408 | tf_op jit(solution)/shard_map/ppermute | solution.py:93
  201.3 5.2 %collective-permute-done.9 = bf16[2,128,448]{1,2,0:T(8,128)(2,1)S(1)} collective-permute-done((bf16[2,128,448]{1,2,0:T(8,128)(2,1)S(1)}, bf16[2,128,448]{1,2,0:T(8,128)(2,1)S(1)}, u32[]{:S(2)}, u32[]{:S(2)}) %collective-permute-start.9) | collective-permute-done | bytes 229408 | tf_op jit(solution)/shard_map/ppermute | solution.py:93
  206.6 0.1 add_convert_fusion
  206.7 3.9 %collective-permute-start.12 = (bf16[128,448]{0,1:T(8,128)(2,1)S(1)}, bf16[128,448]{0,1:T(8,128)(2,1)S(1)}, u32[]{:S(2)}, u32[]{:S(2)}) collective-permute-start(bf16[128,448]{0,1:T(8,128)(2,1)S(1)} %get-tuple-element.48), channel_id=1, source_target_pairs={{0,23},{1,22},{2,21},{3,20},{4,19},{5,18},{6,17},{7,16},{16,7},{17... | collective-permute-start | bytes 344072 | tf_op jit(solution)/shard_map/ppermute | solution.py:18
  210.6 6.0 %collective-permute-start.13 = (bf16[128,448]{0,1:T(8,128)(2,1)S(1)}, bf16[128,448]{0,1:T(8,128)(2,1)S(1)}, u32[]{:S(2)}, u32[]{:S(2)}) collective-permute-start(bf16[128,448]{0,1:T(8,128)(2,1)S(1)} %get-tuple-element.49), channel_id=1, source_target_pairs={{0,19},{1,18},{2,17},{3,16},{4,23},{5,22},{6,21},{7,20},{16,3},{17... | collective-permute-start | bytes 344072 | tf_op jit(solution)/shard_map/ppermute | solution.py:160
  216.6 2.6 %collective-permute-done.12 = bf16[128,448]{0,1:T(8,128)(2,1)S(1)} collective-permute-done((bf16[128,448]{0,1:T(8,128)(2,1)S(1)}, bf16[128,448]{0,1:T(8,128)(2,1)S(1)}, u32[]{:S(2)}, u32[]{:S(2)}) %collective-permute-start.12) | collective-permute-done | bytes 114720 | tf_op jit(solution)/shard_map/ppermute | solution.py:18
  219.2 16.3 %collective-permute-done.13 = bf16[128,448]{0,1:T(8,128)(2,1)S(1)} collective-permute-done((bf16[128,448]{0,1:T(8,128)(2,1)S(1)}, bf16[128,448]{0,1:T(8,128)(2,1)S(1)}, u32[]{:S(2)}, u32[]{:S(2)}) %collective-permute-start.13) | collective-permute-done | bytes 114720 | tf_op jit(solution)/shard_map/ppermute | solution.py:160
  235.5 0.7 fusion.52
  236.2 1.1 copy.21
  (40 shorter events, 0.3 us)
Async XLA Ops:
  0.6 7.1 %copy-start.4 = (bf16[128,3584]{1,0:T(8,128)(2,1)S(1)}, bf16[128,3584]{1,0:T(8,128)(2,1)}, u32[]{:S(2)}) copy-start(bf16[128,3584]{1,0:T(8,128)(2,1)} %param.6) | copy-start | bytes 2752516
  0.6 33.0 %all-to-all-start = ((bf16[16,336,128]{2,1,0:T(8,128)(2,1)}), bf16[16,336,128]{2,1,0:T(8,128)(2,1)S(1)}, u32[]{:S(2)}, u32[]{:S(2)}) async-start(bf16[16,336,128]{2,1,0:T(8,128)(2,1)} %bitcast.112), calls=%async_computation | async-start | bytes 2752512 | tf_op jit(solution)/shard_map/all_to_all | solution.py:131
  8.3 13.4 %copy-start.6 = (s32[32]{0:T(128)S(1)}, s32[32]{0:T(128)}, u32[]{:S(2)}) copy-start(s32[32]{0:T(128)} %param.10) | copy-start | bytes 388
  8.3 13.4 %copy-start.7 = (s32[32]{0:T(128)S(1)}, s32[32]{0:T(128)}, u32[]{:S(2)}) copy-start(s32[32]{0:T(128)} %param.11) | copy-start | bytes 388
  8.4 14.0 %copy-start.8 = (s32[128,2]{0,1:T(2,128)S(1)}, s32[128,2]{0,1:T(2,128)}, u32[]{:S(2)}) copy-start(s32[128,2]{0,1:T(2,128)} %param.7) | copy-start | bytes 3076
  8.4 14.2 %copy-start.5 = (f32[128,2]{0,1:T(2,128)S(1)}, f32[128,2]{0,1:T(2,128)}, u32[]{:S(2)}) copy-start(f32[128,2]{0,1:T(2,128)} %param.8) | copy-start | bytes 3076
  10.6 23.0 %collective-permute-start = (bf16[64,1792]{1,0:T(8,128)(2,1)S(1)}, bf16[64,1792]{1,0:T(8,128)(2,1)S(1)}, u32[]{:S(2)}, u32[]{:S(2)}) collective-permute-start(bf16[64,1792]{1,0:T(8,128)(2,1)S(1)} %constant_dynamic-slice_fusion), channel_id=1, source_target_pairs={{0,23},{1,22},{2,21},{3,20},{4,19},{5,18},{6,17},{7,16},{16,7},{17... | collective-permute-start | bytes 688136 | tf_op jit(solution)/shard_map/ppermute | solution.py:18
  22.6 11.0 %collective-permute-start.1 = (f32[4,128]{1,0:T(4,128)S(1)}, f32[4,128]{1,0:T(4,128)S(1)}, u32[]{:S(2)}, u32[]{:S(2)}) collective-permute-start(f32[4,128]{1,0:T(4,128)S(1)} %pad_maximum_fusion), channel_id=1, source_target_pairs={{0,23},{1,22},{2,21},{3,20},{4,19},{5,18},{6,17},{7,16},{16,7},{17... | collective-permute-start | bytes 6152 | tf_op jit(solution)/shard_map/ppermute | solution.py:18
  33.6 34.1 %all-to-all-start.1 = ((bf16[32,16,1792]{2,1,0:T(8,128)(2,1)}), bf16[32,16,1792]{2,1,0:T(8,128)(2,1)S(1)}, u32[]{:S(2)}, u32[]{:S(2)}) async-start(bf16[32,16,1792]{2,1,0:T(8,128)(2,1)} %bitcast.16), calls=%async_computation.1 | async-start | bytes 3670016 | tf_op jit(solution)/shard_map/all_to_all | solution.py:57
  67.7 1.3 copy-start.3
  69.0 21.4 %copy-start.2 = (bf16[1,3,1792,128]{3,2,1,0:T(8,128)(2,1)S(1)}, bf16[1,3,1792,128]{3,2,1,0:T(8,128)(2,1)}, u32[]{:S(2)}) copy-start(bf16[1,3,1792,128]{3,2,1,0:T(8,128)(2,1)} %param.9) | copy-start | bytes 4128772
  69.0 33.0 %all-to-all-start.2 = ((bf16[32,16,1792]{2,1,0:T(8,128)(2,1)}), bf16[32,16,1792]{2,1,0:T(8,128)(2,1)}, u32[]{:S(2)}, u32[]{:S(2)}) async-start(bf16[32,16,1792]{2,1,0:T(8,128)(2,1)} %bitcast.23), calls=%async_computation.2 | async-start | bytes 3670016 | tf_op jit(solution)/shard_map/all_to_all | solution.py:57
  81.5 14.4 %collective-permute-start.3 = (bf16[336,128]{1,0:T(8,128)(2,1)S(1)}, bf16[336,128]{1,0:T(8,128)(2,1)S(1)}, u32[]{:S(2)}, u32[]{:S(2)}) collective-permute-start(bf16[336,128]{1,0:T(8,128)(2,1)S(1)} %bitcast_select_fusion.1), channel_id=1, source_target_pairs={{0,16},{16,0},{1,17},{17,1},{2,18},{18,2},{3,19},{19,3},{4,20},{20... | collective-permute-start | bytes 258056 | tf_op jit(solution)/shard_map/ppermute | solution.py:14
  92.6 4.7 %collective-permute-start.2 = (f32[2,512,128]{2,1,0:T(8,128)S(1)}, f32[2,512,128]{2,1,0:T(8,128)S(1)}, u32[]{:S(2)}, u32[]{:S(2)}) collective-permute-start(f32[2,512,128]{2,1,0:T(8,128)S(1)} %fusion.6), channel_id=1, source_target_pairs={{0,8},{8,0},{1,9},{9,1},{2,10},{10,2},{3,11},{11,3},{4,12},{12,4},... | collective-permute-start | bytes 1572872 | tf_op jit(solution)/shard_map/ppermute | solution.py:14
  102.0 31.8 %all-to-all-start.3 = ((bf16[32,16,1792]{2,1,0:T(8,128)(2,1)}), bf16[32,16,1792]{2,1,0:T(8,128)(2,1)S(1)}, u32[]{:S(2)}, u32[]{:S(2)}) async-start(bf16[32,16,1792]{2,1,0:T(8,128)(2,1)} %bitcast.110), calls=%async_computation.3 | async-start | bytes 3670016 | tf_op jit(solution)/shard_map/all_to_all | solution.py:57
  111.6 3.8 %collective-permute-start.4 = (f32[2,512,128]{2,1,0:T(8,128)S(1)}, f32[2,512,128]{2,1,0:T(8,128)S(1)}, u32[]{:S(2)}, u32[]{:S(2)}) collective-permute-start(f32[2,512,128]{2,1,0:T(8,128)S(1)} %fusion.9), channel_id=1, source_target_pairs={{0,8},{8,0},{1,9},{9,1},{2,10},{10,2},{3,11},{11,3},{4,12},{12,4},... | collective-permute-start | bytes 1572872 | tf_op jit(solution)/shard_map/ppermute | solution.py:14
  133.8 1.2 copy-start
  135.0 32.5 %all-to-all-start.4 = ((bf16[32,16,1792]{2,1,0:T(8,128)(2,1)}), bf16[32,16,1792]{2,1,0:T(8,128)(2,1)S(1)}, u32[]{:S(2)}, u32[]{:S(2)}) async-start(bf16[32,16,1792]{2,1,0:T(8,128)(2,1)} %bitcast.109), calls=%async_computation.4 | async-start | bytes 3670016 | tf_op jit(solution)/shard_map/all_to_all | solution.py:57
  141.6 2.4 %copy-start.1 = (bf16[32,16,1792]{2,1,0:T(8,128)(2,1)S(1)}, bf16[32,16,1792]{2,1,0:T(8,128)(2,1)}, u32[]{:S(2)}) copy-start(bf16[32,16,1792]{2,1,0:T(8,128)(2,1)} %copy-done) | copy-start | bytes 5505028
  153.5 33.8 %collective-permute-start.5 = (bf16[2,128,448]{1,2,0:T(8,128)(2,1)}, bf16[2,128,448]{1,2,0:T(8,128)(2,1)}, u32[]{:S(2)}, u32[]{:S(2)}) collective-permute-start(bf16[2,128,448]{1,2,0:T(8,128)(2,1)} %get-tuple-element.40), channel_id=1, source_target_pairs={{0,1},{1,0},{2,3},{3,2},{4,5},{5,4},{6,7},{7,6},{8,9},{9,8},{10,11... | collective-permute-start | bytes 688136 | tf_op jit(solution)/shard_map/ppermute | solution.py:93
  155.5 34.1 %collective-permute-start.6 = (bf16[2,128,448]{1,2,0:T(8,128)(2,1)S(1)}, bf16[2,128,448]{1,2,0:T(8,128)(2,1)}, u32[]{:S(2)}, u32[]{:S(2)}) collective-permute-start(bf16[2,128,448]{1,2,0:T(8,128)(2,1)S(1)} %get-tuple-element.42), channel_id=1, source_target_pairs={{0,2},{1,3},{2,0},{3,1},{4,6},{5,7},{6,4},{7,5},{8,10},{9,11},{10,... | collective-permute-start | bytes 688136 | tf_op jit(solution)/shard_map/ppermute | solution.py:93
  165.5 24.0 %collective-permute-start.7 = (bf16[2,128,448]{1,2,0:T(8,128)(2,1)S(1)}, bf16[2,128,448]{1,2,0:T(8,128)(2,1)}, u32[]{:S(2)}, u32[]{:S(2)}) collective-permute-start(bf16[2,128,448]{1,2,0:T(8,128)(2,1)S(1)} %get-tuple-element.41), channel_id=1, source_target_pairs={{0,3},{1,2},{2,1},{3,0},{4,7},{5,6},{6,5},{7,4},{8,11},{9,10},{10,... | collective-permute-start | bytes 688136 | tf_op jit(solution)/shard_map/ppermute | solution.py:93
  172.1 64.1 %all-to-all-start.5 = ((bf16[16,336,128]{2,1,0:T(8,128)(2,1)}), bf16[16,336,128]{2,1,0:T(8,128)(2,1)S(1)}, u32[]{:S(2)}, u32[]{:S(2)}) async-start(bf16[16,336,128]{2,1,0:T(8,128)(2,1)} %select_select_fusion), calls=%async_computation.5 | async-start | bytes 2752512 | tf_op jit(solution)/shard_map/all_to_all | solution.py:152
  178.9 22.4 %collective-permute-start.10 = (bf16[2,128,448]{1,2,0:T(8,128)(2,1)S(1)}, bf16[2,128,448]{1,2,0:T(8,128)(2,1)S(1)}, u32[]{:S(2)}, u32[]{:S(2)}) collective-permute-start(bf16[2,128,448]{1,2,0:T(8,128)(2,1)S(1)} %get-tuple-element.46), channel_id=1, source_target_pairs={{0,2},{1,3},{2,0},{3,1},{4,6},{5,7},{6,4},{7,5},{8,10},{9,11},{10,... | collective-permute-start | bytes 688136 | tf_op jit(solution)/shard_map/ppermute | solution.py:93
  182.0 19.3 %collective-permute-start.11 = (bf16[2,128,448]{1,2,0:T(8,128)(2,1)S(1)}, bf16[2,128,448]{1,2,0:T(8,128)(2,1)S(1)}, u32[]{:S(2)}, u32[]{:S(2)}) collective-permute-start(bf16[2,128,448]{1,2,0:T(8,128)(2,1)S(1)} %get-tuple-element.45), channel_id=1, source_target_pairs={{0,3},{1,2},{2,1},{3,0},{4,7},{5,6},{6,5},{7,4},{8,11},{9,10},{10,... | collective-permute-start | bytes 688136 | tf_op jit(solution)/shard_map/ppermute | solution.py:93
  187.3 19.2 %collective-permute-start.9 = (bf16[2,128,448]{1,2,0:T(8,128)(2,1)S(1)}, bf16[2,128,448]{1,2,0:T(8,128)(2,1)S(1)}, u32[]{:S(2)}, u32[]{:S(2)}) collective-permute-start(bf16[2,128,448]{1,2,0:T(8,128)(2,1)S(1)} %get-tuple-element.47), channel_id=1, source_target_pairs={{0,1},{1,0},{2,3},{3,2},{4,5},{5,4},{6,7},{7,6},{8,9},{9,8},{10,11... | collective-permute-start | bytes 688136 | tf_op jit(solution)/shard_map/ppermute | solution.py:93
  190.8 25.7 %collective-permute-start.8 = (bf16[128,448]{0,1:T(8,128)(2,1)S(1)}, bf16[128,448]{0,1:T(8,128)(2,1)S(1)}, u32[]{:S(2)}, u32[]{:S(2)}) collective-permute-start(bf16[128,448]{0,1:T(8,128)(2,1)S(1)} %dynamic-slice_bitcast_fusion.10), channel_id=1, source_target_pairs={{0,4},{4,0},{1,5},{5,1},{2,6},{6,2},{3,7},{7,3},{8,12},{12,8},{9,1... | collective-permute-start | bytes 344072 | tf_op jit(solution)/shard_map/ppermute | solution.py:14
  206.7 12.4 %collective-permute-start.12 = (bf16[128,448]{0,1:T(8,128)(2,1)S(1)}, bf16[128,448]{0,1:T(8,128)(2,1)S(1)}, u32[]{:S(2)}, u32[]{:S(2)}) collective-permute-start(bf16[128,448]{0,1:T(8,128)(2,1)S(1)} %get-tuple-element.48), channel_id=1, source_target_pairs={{0,23},{1,22},{2,21},{3,20},{4,19},{5,18},{6,17},{7,16},{16,7},{17... | collective-permute-start | bytes 344072 | tf_op jit(solution)/shard_map/ppermute | solution.py:18
  210.6 24.9 %collective-permute-start.13 = (bf16[128,448]{0,1:T(8,128)(2,1)S(1)}, bf16[128,448]{0,1:T(8,128)(2,1)S(1)}, u32[]{:S(2)}, u32[]{:S(2)}) collective-permute-start(bf16[128,448]{0,1:T(8,128)(2,1)S(1)} %get-tuple-element.49), channel_id=1, source_target_pairs={{0,19},{1,18},{2,17},{3,16},{4,23},{5,22},{6,21},{7,20},{16,3},{17... | collective-permute-start | bytes 344072 | tf_op jit(solution)/shard_map/ppermute | solution.py:160
where the time goes:
time: 238 us; the launch traced here: 237 us
  starting transfers between devices  113 us (47%)
  waiting for transfers between devices  58.2 us (24%)
  blocking collectives  21.5 us (9%)
  matrix products  17.6 us (7%)
  local copies, waits for them, and re-layouts  17.5 us (7%)
  other arithmetic  5.65 us (2%)
  between operations  3.79 us (2%)
    all_to_all x4, starting transfers between devices, exchange(): lax.all_to_all(blocks, axes, split_axis=0, concat_axis=0, tiled=True)  32.3 us
    ppermute x6, starting transfers between devices, near_sum(): lax.ppermute(block, NEAR, [(i, i ^ step) for i in range(count)])  24.5 us
    all_gather x1, blocking collectives, shards(): other_table = lax.all_gather(quarter, NEAR, tiled=True)  21.5 us
    all_to_all x4, waiting for transfers between devices, exchange(): lax.all_to_all(blocks, axes, split_axis=0, concat_axis=0, tiled=True)  20 us
    ppermute x4, starting transfers between devices, swap(): return lax.ppermute(value, axis, [(0, 1), (1, 0)])  19.6 us
    ppermute x3, starting transfers between devices, mirrored(): return lax.ppermute(value, RING, [(i, 15 - i) for i in range(16)])  16.9 us
    ppermute x1, waiting for transfers between devices, shards(): lax.ppermute(of(other_kept, far), RING, [(i, i ^ 11) for i in range(16)])  16.3 us
    ppermute x6, waiting for transfers between devices, near_sum(): lax.ppermute(block, NEAR, [(i, i ^ step) for i in range(count)])  9.81 us
  transfers between devices with their start and end apart: 20, of which 10 were waited for; matrix products, arithmetic and copies ran while one was open for 16% of the time, Pallas kernels for 0%

commit v1 on v0

--- a/solution.py
+++ b/solution.py
@@ -137,7 +137,10 @@
     )
     sent = exchange(payload)
     other_rows = placed_rows(other_codes, zh)
-    other_table = lax.all_gather(quarter, NEAR, tiled=True)
+    n_dev = lax.axis_size(NEAR)
+    pieces = jnp.stack([quarter for _ in range(n_dev)])
+    pieces = lax.all_to_all(pieces, NEAR, split_axis=0, concat_axis=0)
+    other_table = jnp.concatenate(pieces, axis=0)
     payload, sent = tied((gather_rows(other_rows, other_table), sent))
     other_sent = exchange(payload)
     chosen = pick_pieces(spread, old_owner, new_owner, zh)

time: 238 us -> 262 us (1.10)
  waiting for transfers between devices: 58.2 us -> 83.3 us
  blocking collectives: 21.5 us -> 30.6 us
  starting transfers between devices: 113 us -> 104 us
    all_to_all x0 -> x1, blocking collectives: none -> 30.6 us  [shards(): pieces = lax.all_to_all(pieces, NEAR, split_axis=0, concat_axis=0)]
    all_to_all x4, waiting for transfers between devices: 20 us -> 42.8 us  [exchange(): lax.all_to_all(blocks, axes, split_axis=0, concat_axis=0, tiled=True)]
    all_gather x1 -> x0, blocking collectives: 21.5 us -> none  [shards(): other_table = lax.all_gather(quarter, NEAR, tiled=True)]
    all_to_all x4, starting transfers between devices: 32.3 us -> 28.5 us  [exchange(): lax.all_to_all(blocks, axes, split_axis=0, concat_axis=0, tiled=True)]
  transfers between devices with their start and end apart: 20 -> 20, of which waited for: 10 -> 11; matrix products, arithmetic and copies ran while one was open for 16% -> 14% of each run, Pallas kernels for 0% -> 0%
where the time goes in v1:
time: 262 us; the launch traced here: 261 us
  starting transfers between devices  104 us (40%)
  waiting for transfers between devices  83.3 us (32%)
  blocking collectives  30.6 us (12%)
  matrix products  17.6 us (7%)
  local copies, waits for them, and re-layouts  16.2 us (6%)
  other arithmetic  5.65 us (2%)
  between operations  3.78 us (1%)
    all_to_all x4, waiting for transfers between devices, exchange(): lax.all_to_all(blocks, axes, split_axis=0, concat_axis=0, tiled=True)  42.8 us
    all_to_all x1, blocking collectives, shards(): pieces = lax.all_to_all(pieces, NEAR, split_axis=0, concat_axis=0)  30.6 us
    all_to_all x4, starting transfers between devices, exchange(): lax.all_to_all(blocks, axes, split_axis=0, concat_axis=0, tiled=True)  28.5 us
    ppermute x6, starting transfers between devices, near_sum(): lax.ppermute(block, NEAR, [(i, i ^ step) for i in range(count)])  22 us
    ppermute x3, starting transfers between devices, mirrored(): return lax.ppermute(value, RING, [(i, 15 - i) for i in range(16)])  18.8 us
    ppermute x4, starting transfers between devices, swap(): return lax.ppermute(value, axis, [(0, 1), (1, 0)])  18.1 us
    ppermute x1, waiting for transfers between devices, shards(): lax.ppermute(of(other_kept, far), RING, [(i, i ^ 11) for i in range(16)])  15.6 us
    ppermute x6, waiting for transfers between devices, near_sum(): lax.ppermute(block, NEAR, [(i, i ^ step) for i in range(count)])  11.4 us
  transfers between devices with their start and end apart: 20, of which 11 were waited for; matrix products, arithmetic and copies ran while one was open for 14% of the time, Pallas kernels for 0%

profile of v1, /device:TPU:99, one launch (start us, length us, event | category | flops | bytes accessed | tf_op | source)
XLA Modules:
  0.0 260.9 jit_solution(18120433896649765108)
XLA Ops:
  0.6 7.1 %all-to-all-start = ((bf16[16,336,128]{2,1,0:T(8,128)(2,1)}), bf16[16,336,128]{2,1,0:T(8,128)(2,1)S(1)}, u32[]{:S(2)}, u32[]{:S(2)}) async-start(bf16[16,336,128]{2,1,0:T(8,128)(2,1)} %bitcast.113), calls=%async_computation | async-start | bytes 2752512 | tf_op jit(solution)/shard_map/all_to_all | solution.py:131
  7.7 0.6 copy.9
  8.4 0.9 copy.16
  9.3 1.3 reshape.280
  10.6 11.1 %collective-permute-start = (bf16[64,1792]{1,0:T(8,128)(2,1)S(1)}, bf16[64,1792]{1,0:T(8,128)(2,1)S(1)}, u32[]{:S(2)}, u32[]{:S(2)}) collective-permute-start(bf16[64,1792]{1,0:T(8,128)(2,1)S(1)} %constant_dynamic-slice_fusion), channel_id=1, source_target_pairs={{0,23},{1,22},{2,21},{3,20},{4,19},{5,18},{6,17},{7,16},{16,7},{17... | collective-permute-start | bytes 688136 | tf_op jit(solution)/shard_map/ppermute | solution.py:18
  21.7 0.6 fusion.67
  22.4 0.2 fusion.13
  22.6 1.9 collective-permute-start.1
  24.6 1.9 convolution_convert_fusion.1
  26.5 7.1 %collective-permute-done.1 = f32[4,128]{1,0:T(4,128)S(1)} collective-permute-done((f32[4,128]{1,0:T(4,128)S(1)}, f32[4,128]{1,0:T(4,128)S(1)}, u32[]{:S(2)}, u32[]{:S(2)}) %collective-permute-start.1) | collective-permute-done | bytes 2080 | tf_op jit(solution)/shard_map/ppermute | solution.py:18
  33.6 0.1 stack.25
  33.7 30.6 %all_to_all.35 = bf16[4,64,1792]{2,1,0:T(8,128)(2,1)S(1)} all-to-all(bf16[4,64,1792]{2,1,0:T(8,128)(2,1)S(1)} %stack.25), channel_id=1, replica_groups=mesh['y'=4,'x'=4,'zh'=2,'c'=2,'ma'=2,'mb'=2,'mc'=2] {'mb','mc'}, dimensions={0} | all-to-all | bytes 1835008 | tf_op jit(solution)/shard_map/all_to_all | solution.py:142
  64.3 8.2 %all-to-all-start.2 = ((bf16[32,16,1792]{2,1,0:T(8,128)(2,1)}), bf16[32,16,1792]{2,1,0:T(8,128)(2,1)}, u32[]{:S(2)}, u32[]{:S(2)}) async-start(bf16[32,16,1792]{2,1,0:T(8,128)(2,1)} %bitcast.17), calls=%async_computation.2 | async-start | bytes 3670016 | tf_op jit(solution)/shard_map/all_to_all | solution.py:57
  72.5 1.9 convolution_convert_fusion
  74.4 22.5 %all-to-all-done.2 = bf16[32,16,1792]{2,1,0:T(8,128)(2,1)} async-done(((bf16[32,16,1792]{2,1,0:T(8,128)(2,1)}), bf16[32,16,1792]{2,1,0:T(8,128)(2,1)}, u32[]{:S(2)}, u32[]{:S(2)}) %all-to-all-start.2) | async-done | bytes 1835040 | tf_op jit(solution)/shard_map/all_to_all | solution.py:57
  96.9 7.3 %all-to-all-start.3 = ((bf16[32,16,1792]{2,1,0:T(8,128)(2,1)}), bf16[32,16,1792]{2,1,0:T(8,128)(2,1)}, u32[]{:S(2)}, u32[]{:S(2)}) async-start(bf16[32,16,1792]{2,1,0:T(8,128)(2,1)} %bitcast.24), calls=%async_computation.3 | async-start | bytes 3670016 | tf_op jit(solution)/shard_map/all_to_all | solution.py:57
  106.8 1.3 fusion.69
  108.1 8.0 %collective-permute-start.3 = (bf16[336,128]{1,0:T(8,128)(2,1)S(1)}, bf16[336,128]{1,0:T(8,128)(2,1)S(1)}, u32[]{:S(2)}, u32[]{:S(2)}) collective-permute-start(bf16[336,128]{1,0:T(8,128)(2,1)S(1)} %bitcast_select_fusion.1), channel_id=1, source_target_pairs={{0,16},{16,0},{1,17},{17,1},{2,18},{18,2},{3,19},{19,3},{4,20},{20... | collective-permute-start | bytes 258056 | tf_op jit(solution)/shard_map/ppermute | solution.py:14
  116.1 2.1 fusion.6
  118.2 2.5 collective-permute-start.2
  120.8 1.7 collective-permute-done.3
  122.5 1.3 select_select_fusion
  123.9 1.9 convolution_convert_fusion.3
  125.8 2.9 %all-to-all-done.3 = bf16[32,16,1792]{2,1,0:T(8,128)(2,1)} async-done(((bf16[32,16,1792]{2,1,0:T(8,128)(2,1)}), bf16[32,16,1792]{2,1,0:T(8,128)(2,1)}, u32[]{:S(2)}, u32[]{:S(2)}) %all-to-all-start.3) | async-done | bytes 1835040 | tf_op jit(solution)/shard_map/all_to_all | solution.py:57
  128.7 6.5 %all-to-all-start.4 = ((bf16[32,16,1792]{2,1,0:T(8,128)(2,1)}), bf16[32,16,1792]{2,1,0:T(8,128)(2,1)S(1)}, u32[]{:S(2)}, u32[]{:S(2)}) async-start(bf16[32,16,1792]{2,1,0:T(8,128)(2,1)} %bitcast.111), calls=%async_computation.4 | async-start | bytes 3670016 | tf_op jit(solution)/shard_map/all_to_all | solution.py:57
  135.2 2.1 fusion.9
  137.3 2.3 collective-permute-start.4
  139.6 1.5 collective-permute-done.4
  141.1 0.1 add.237
  141.2 1.9 convolution_convert_fusion.2
  143.1 16.5 %all-to-all-done.4 = bf16[32,16,1792]{2,1,0:T(8,128)(2,1)S(1)} async-done(((bf16[32,16,1792]{2,1,0:T(8,128)(2,1)}), bf16[32,16,1792]{2,1,0:T(8,128)(2,1)S(1)}, u32[]{:S(2)}, u32[]{:S(2)}) %all-to-all-start.4) | async-done | bytes 1835040 | tf_op jit(solution)/shard_map/all_to_all | solution.py:57
  159.6 1.2 copy-done
  160.8 6.5 %all-to-all-start.5 = ((bf16[32,16,1792]{2,1,0:T(8,128)(2,1)}), bf16[32,16,1792]{2,1,0:T(8,128)(2,1)S(1)}, u32[]{:S(2)}, u32[]{:S(2)}) async-start(bf16[32,16,1792]{2,1,0:T(8,128)(2,1)} %bitcast.110), calls=%async_computation.5 | async-start | bytes 3670016 | tf_op jit(solution)/shard_map/all_to_all | solution.py:57
  167.4 2.4 fusion.45
  169.8 1.7 fusion
  171.5 3.5 %reshape.281 = bf16[2,128,2,4,224]{4,3,2,1,0:T(4,128)(2,1)S(1)} reshape(bf16[256,1792]{1,0:T(8,128)(2,1)} %fusion) | data formatting | bytes 1835008 | tf_op jit(solution)/shard_map/reshape | solution.py:82
  175.0 2.3 copy.18
  177.3 1.3 copy.13
  178.6 0.8 dynamic-slice_bitcast_fusion.6
  179.3 1.9 collective-permute-start.5
  181.3 7.6 %collective-permute-start.6 = (bf16[2,128,448]{1,2,0:T(8,128)(2,1)S(1)}, bf16[2,128,448]{1,2,0:T(8,128)(2,1)}, u32[]{:S(2)}, u32[]{:S(2)}) collective-permute-start(bf16[2,128,448]{1,2,0:T(8,128)(2,1)S(1)} %get-tuple-element.42), channel_id=1, source_target_pairs={{0,2},{1,3},{2,0},{3,1},{4,6},{5,7},{6,4},{7,5},{8,10},{9,11},{10,... | collective-permute-start | bytes 688136 | tf_op jit(solution)/shard_map/ppermute | solution.py:93
  188.9 1.9 collective-permute-start.7
  190.8 0.9 all-to-all-done.5
  191.7 0.8 fusion.48
  192.5 0.8 fusion.1
  193.3 1.5 reshape.282
  194.7 1.4 copy.19
  196.2 0.1 copy.15
  196.3 0.1 dynamic-slice_bitcast_fusion.3
  196.4 5.9 %all-to-all-start.6 = ((bf16[16,336,128]{2,1,0:T(8,128)(2,1)}), bf16[16,336,128]{2,1,0:T(8,128)(2,1)S(1)}, u32[]{:S(2)}, u32[]{:S(2)}) async-start(bf16[16,336,128]{2,1,0:T(8,128)(2,1)} %select_select_fusion), calls=%async_computation.6 | async-start | bytes 2752512 | tf_op jit(solution)/shard_map/all_to_all | solution.py:155
  202.2 5.4 %collective-permute-start.10 = (bf16[2,128,448]{1,2,0:T(8,128)(2,1)S(1)}, bf16[2,128,448]{1,2,0:T(8,128)(2,1)S(1)}, u32[]{:S(2)}, u32[]{:S(2)}) collective-permute-start(bf16[2,128,448]{1,2,0:T(8,128)(2,1)S(1)} %get-tuple-element.46), channel_id=1, source_target_pairs={{0,2},{1,3},{2,0},{3,1},{4,6},{5,7},{6,4},{7,5},{8,10},{9,11},{10,... | collective-permute-start | bytes 688136 | tf_op jit(solution)/shard_map/ppermute | solution.py:93
  207.6 3.1 %collective-permute-start.11 = (bf16[2,128,448]{1,2,0:T(8,128)(2,1)S(1)}, bf16[2,128,448]{1,2,0:T(8,128)(2,1)S(1)}, u32[]{:S(2)}, u32[]{:S(2)}) collective-permute-start(bf16[2,128,448]{1,2,0:T(8,128)(2,1)S(1)} %get-tuple-element.45), channel_id=1, source_target_pairs={{0,3},{1,2},{2,1},{3,0},{4,7},{5,6},{6,5},{7,4},{8,11},{9,10},{10,... | collective-permute-start | bytes 688136 | tf_op jit(solution)/shard_map/ppermute | solution.py:93
  210.7 2.2 collective-permute-start.9
  212.9 1.3 add_convert_fusion.1
  214.2 5.3 %collective-permute-start.8 = (bf16[128,448]{0,1:T(8,128)(2,1)S(1)}, bf16[128,448]{0,1:T(8,128)(2,1)S(1)}, u32[]{:S(2)}, u32[]{:S(2)}) collective-permute-start(bf16[128,448]{0,1:T(8,128)(2,1)S(1)} %dynamic-slice_bitcast_fusion.10), channel_id=1, source_target_pairs={{0,4},{4,0},{1,5},{5,1},{2,6},{6,2},{3,7},{7,3},{8,12},{12,8},{9,1... | collective-permute-start | bytes 344072 | tf_op jit(solution)/shard_map/ppermute | solution.py:14
  219.6 4.7 %collective-permute-done.10 = bf16[2,128,448]{1,2,0:T(8,128)(2,1)S(1)} collective-permute-done((bf16[2,128,448]{1,2,0:T(8,128)(2,1)S(1)}, bf16[2,128,448]{1,2,0:T(8,128)(2,1)S(1)}, u32[]{:S(2)}, u32[]{:S(2)}) %collective-permute-start.10) | collective-permute-done | bytes 229408 | tf_op jit(solution)/shard_map/ppermute | solution.py:93
  224.2 6.7 %collective-permute-done.9 = bf16[2,128,448]{1,2,0:T(8,128)(2,1)S(1)} collective-permute-done((bf16[2,128,448]{1,2,0:T(8,128)(2,1)S(1)}, bf16[2,128,448]{1,2,0:T(8,128)(2,1)S(1)}, u32[]{:S(2)}, u32[]{:S(2)}) %collective-permute-start.9) | collective-permute-done | bytes 229408 | tf_op jit(solution)/shard_map/ppermute | solution.py:93
  230.9 0.1 add_convert_fusion
  231.1 5.8 %collective-permute-start.12 = (bf16[128,448]{0,1:T(8,128)(2,1)S(1)}, bf16[128,448]{0,1:T(8,128)(2,1)S(1)}, u32[]{:S(2)}, u32[]{:S(2)}) collective-permute-start(bf16[128,448]{0,1:T(8,128)(2,1)S(1)} %get-tuple-element.48), channel_id=1, source_target_pairs={{0,23},{1,22},{2,21},{3,20},{4,19},{5,18},{6,17},{7,16},{16,7},{17... | collective-permute-start | bytes 344072 | tf_op jit(solution)/shard_map/ppermute | solution.py:18
  236.8 3.4 %collective-permute-start.13 = (bf16[128,448]{0,1:T(8,128)(2,1)S(1)}, bf16[128,448]{0,1:T(8,128)(2,1)S(1)}, u32[]{:S(2)}, u32[]{:S(2)}) collective-permute-start(bf16[128,448]{0,1:T(8,128)(2,1)S(1)} %get-tuple-element.49), channel_id=1, source_target_pairs={{0,19},{1,18},{2,17},{3,16},{4,23},{5,22},{6,21},{7,20},{16,3},{17... | collective-permute-start | bytes 344072 | tf_op jit(solution)/shard_map/ppermute | solution.py:163
  240.2 3.3 %collective-permute-done.12 = bf16[128,448]{0,1:T(8,128)(2,1)S(1)} collective-permute-done((bf16[128,448]{0,1:T(8,128)(2,1)S(1)}, bf16[128,448]{0,1:T(8,128)(2,1)S(1)}, u32[]{:S(2)}, u32[]{:S(2)}) %collective-permute-start.12) | collective-permute-done | bytes 114720 | tf_op jit(solution)/shard_map/ppermute | solution.py:18
  243.5 15.6 %collective-permute-done.13 = bf16[128,448]{0,1:T(8,128)(2,1)S(1)} collective-permute-done((bf16[128,448]{0,1:T(8,128)(2,1)S(1)}, bf16[128,448]{0,1:T(8,128)(2,1)S(1)}, u32[]{:S(2)}, u32[]{:S(2)}) %collective-permute-start.13) | collective-permute-done | bytes 114720 | tf_op jit(solution)/shard_map/ppermute | solution.py:163
  259.1 0.7 fusion.52
  259.8 1.1 copy.21
  (39 shorter events, 0.3 us)
Async XLA Ops:
  0.6 7.1 %copy-start.3 = (bf16[128,3584]{1,0:T(8,128)(2,1)S(1)}, bf16[128,3584]{1,0:T(8,128)(2,1)}, u32[]{:S(2)}) copy-start(bf16[128,3584]{1,0:T(8,128)(2,1)} %param.6) | copy-start | bytes 2752516
  0.6 33.0 %all-to-all-start = ((bf16[16,336,128]{2,1,0:T(8,128)(2,1)}), bf16[16,336,128]{2,1,0:T(8,128)(2,1)S(1)}, u32[]{:S(2)}, u32[]{:S(2)}) async-start(bf16[16,336,128]{2,1,0:T(8,128)(2,1)} %bitcast.113), calls=%async_computation | async-start | bytes 2752512 | tf_op jit(solution)/shard_map/all_to_all | solution.py:131
  8.3 13.4 %copy-start.5 = (s32[32]{0:T(128)S(1)}, s32[32]{0:T(128)}, u32[]{:S(2)}) copy-start(s32[32]{0:T(128)} %param.10) | copy-start | bytes 388
  8.3 13.4 %copy-start.6 = (s32[32]{0:T(128)S(1)}, s32[32]{0:T(128)}, u32[]{:S(2)}) copy-start(s32[32]{0:T(128)} %param.11) | copy-start | bytes 388
  8.4 14.0 %copy-start.7 = (s32[128,2]{0,1:T(2,128)S(1)}, s32[128,2]{0,1:T(2,128)}, u32[]{:S(2)}) copy-start(s32[128,2]{0,1:T(2,128)} %param.7) | copy-start | bytes 3076
  8.4 14.2 %copy-start.4 = (f32[128,2]{0,1:T(2,128)S(1)}, f32[128,2]{0,1:T(2,128)}, u32[]{:S(2)}) copy-start(f32[128,2]{0,1:T(2,128)} %param.8) | copy-start | bytes 3076
  10.6 23.0 %collective-permute-start = (bf16[64,1792]{1,0:T(8,128)(2,1)S(1)}, bf16[64,1792]{1,0:T(8,128)(2,1)S(1)}, u32[]{:S(2)}, u32[]{:S(2)}) collective-permute-start(bf16[64,1792]{1,0:T(8,128)(2,1)S(1)} %constant_dynamic-slice_fusion), channel_id=1, source_target_pairs={{0,23},{1,22},{2,21},{3,20},{4,19},{5,18},{6,17},{7,16},{16,7},{17... | collective-permute-start | bytes 688136 | tf_op jit(solution)/shard_map/ppermute | solution.py:18
  22.6 11.0 %collective-permute-start.1 = (f32[4,128]{1,0:T(4,128)S(1)}, f32[4,128]{1,0:T(4,128)S(1)}, u32[]{:S(2)}, u32[]{:S(2)}) collective-permute-start(f32[4,128]{1,0:T(4,128)S(1)} %pad_maximum_fusion), channel_id=1, source_target_pairs={{0,23},{1,22},{2,21},{3,20},{4,19},{5,18},{6,17},{7,16},{16,7},{17... | collective-permute-start | bytes 6152 | tf_op jit(solution)/shard_map/ppermute | solution.py:18
  64.3 32.6 %all-to-all-start.2 = ((bf16[32,16,1792]{2,1,0:T(8,128)(2,1)}), bf16[32,16,1792]{2,1,0:T(8,128)(2,1)}, u32[]{:S(2)}, u32[]{:S(2)}) async-start(bf16[32,16,1792]{2,1,0:T(8,128)(2,1)} %bitcast.17), calls=%async_computation.2 | async-start | bytes 3670016 | tf_op jit(solution)/shard_map/all_to_all | solution.py:57
  96.9 19.2 %copy-start.2 = (bf16[1,3,1792,128]{3,2,1,0:T(8,128)(2,1)S(1)}, bf16[1,3,1792,128]{3,2,1,0:T(8,128)(2,1)}, u32[]{:S(2)}) copy-start(bf16[1,3,1792,128]{3,2,1,0:T(8,128)(2,1)} %param.9) | copy-start | bytes 4128772
  96.9 31.8 %all-to-all-start.3 = ((bf16[32,16,1792]{2,1,0:T(8,128)(2,1)}), bf16[32,16,1792]{2,1,0:T(8,128)(2,1)}, u32[]{:S(2)}, u32[]{:S(2)}) async-start(bf16[32,16,1792]{2,1,0:T(8,128)(2,1)} %bitcast.24), calls=%async_computation.3 | async-start | bytes 3670016 | tf_op jit(solution)/shard_map/all_to_all | solution.py:57
  108.1 14.4 %collective-permute-start.3 = (bf16[336,128]{1,0:T(8,128)(2,1)S(1)}, bf16[336,128]{1,0:T(8,128)(2,1)S(1)}, u32[]{:S(2)}, u32[]{:S(2)}) collective-permute-start(bf16[336,128]{1,0:T(8,128)(2,1)S(1)} %bitcast_select_fusion.1), channel_id=1, source_target_pairs={{0,16},{16,0},{1,17},{17,1},{2,18},{18,2},{3,19},{19,3},{4,20},{20... | collective-permute-start | bytes 258056 | tf_op jit(solution)/shard_map/ppermute | solution.py:14
  118.2 5.6 %collective-permute-start.2 = (f32[2,512,128]{2,1,0:T(8,128)S(1)}, f32[2,512,128]{2,1,0:T(8,128)S(1)}, u32[]{:S(2)}, u32[]{:S(2)}) collective-permute-start(f32[2,512,128]{2,1,0:T(8,128)S(1)} %fusion.6), channel_id=1, source_target_pairs={{0,8},{8,0},{1,9},{9,1},{2,10},{10,2},{3,11},{11,3},{4,12},{12,4},... | collective-permute-start | bytes 1572872 | tf_op jit(solution)/shard_map/ppermute | solution.py:14
  128.7 30.9 %all-to-all-start.4 = ((bf16[32,16,1792]{2,1,0:T(8,128)(2,1)}), bf16[32,16,1792]{2,1,0:T(8,128)(2,1)S(1)}, u32[]{:S(2)}, u32[]{:S(2)}) async-start(bf16[32,16,1792]{2,1,0:T(8,128)(2,1)} %bitcast.111), calls=%async_computation.4 | async-start | bytes 3670016 | tf_op jit(solution)/shard_map/all_to_all | solution.py:57
  137.3 3.8 %collective-permute-start.4 = (f32[2,512,128]{2,1,0:T(8,128)S(1)}, f32[2,512,128]{2,1,0:T(8,128)S(1)}, u32[]{:S(2)}, u32[]{:S(2)}) collective-permute-start(f32[2,512,128]{2,1,0:T(8,128)S(1)} %fusion.9), channel_id=1, source_target_pairs={{0,8},{8,0},{1,9},{9,1},{2,10},{10,2},{3,11},{11,3},{4,12},{12,4},... | collective-permute-start | bytes 1572872 | tf_op jit(solution)/shard_map/ppermute | solution.py:14
  159.6 1.2 copy-start
  160.8 30.9 %all-to-all-start.5 = ((bf16[32,16,1792]{2,1,0:T(8,128)(2,1)}), bf16[32,16,1792]{2,1,0:T(8,128)(2,1)S(1)}, u32[]{:S(2)}, u32[]{:S(2)}) async-start(bf16[32,16,1792]{2,1,0:T(8,128)(2,1)} %bitcast.110), calls=%async_computation.5 | async-start | bytes 3670016 | tf_op jit(solution)/shard_map/all_to_all | solution.py:57
  167.4 2.4 copy-start.1
  179.3 31.3 %collective-permute-start.5 = (bf16[2,128,448]{1,2,0:T(8,128)(2,1)}, bf16[2,128,448]{1,2,0:T(8,128)(2,1)}, u32[]{:S(2)}, u32[]{:S(2)}) collective-permute-start(bf16[2,128,448]{1,2,0:T(8,128)(2,1)} %get-tuple-element.40), channel_id=1, source_target_pairs={{0,1},{1,0},{2,3},{3,2},{4,5},{5,4},{6,7},{7,6},{8,9},{9,8},{10,11... | collective-permute-start | bytes 688136 | tf_op jit(solution)/shard_map/ppermute | solution.py:93
  181.3 31.6 %collective-permute-start.6 = (bf16[2,128,448]{1,2,0:T(8,128)(2,1)S(1)}, bf16[2,128,448]{1,2,0:T(8,128)(2,1)}, u32[]{:S(2)}, u32[]{:S(2)}) collective-permute-start(bf16[2,128,448]{1,2,0:T(8,128)(2,1)S(1)} %get-tuple-element.42), channel_id=1, source_target_pairs={{0,2},{1,3},{2,0},{3,1},{4,6},{5,7},{6,4},{7,5},{8,10},{9,11},{10,... | collective-permute-start | bytes 688136 | tf_op jit(solution)/shard_map/ppermute | solution.py:93
  188.9 24.0 %collective-permute-start.7 = (bf16[2,128,448]{1,2,0:T(8,128)(2,1)S(1)}, bf16[2,128,448]{1,2,0:T(8,128)(2,1)}, u32[]{:S(2)}, u32[]{:S(2)}) collective-permute-start(bf16[2,128,448]{1,2,0:T(8,128)(2,1)S(1)} %get-tuple-element.41), channel_id=1, source_target_pairs={{0,3},{1,2},{2,1},{3,0},{4,7},{5,6},{6,5},{7,4},{8,11},{9,10},{10,... | collective-permute-start | bytes 688136 | tf_op jit(solution)/shard_map/ppermute | solution.py:93
  196.4 63.4 %all-to-all-start.6 = ((bf16[16,336,128]{2,1,0:T(8,128)(2,1)}), bf16[16,336,128]{2,1,0:T(8,128)(2,1)S(1)}, u32[]{:S(2)}, u32[]{:S(2)}) async-start(bf16[16,336,128]{2,1,0:T(8,128)(2,1)} %select_select_fusion), calls=%async_computation.6 | async-start | bytes 2752512 | tf_op jit(solution)/shard_map/all_to_all | solution.py:155
  202.2 22.0 %collective-permute-start.10 = (bf16[2,128,448]{1,2,0:T(8,128)(2,1)S(1)}, bf16[2,128,448]{1,2,0:T(8,128)(2,1)S(1)}, u32[]{:S(2)}, u32[]{:S(2)}) collective-permute-start(bf16[2,128,448]{1,2,0:T(8,128)(2,1)S(1)} %get-tuple-element.46), channel_id=1, source_target_pairs={{0,2},{1,3},{2,0},{3,1},{4,6},{5,7},{6,4},{7,5},{8,10},{9,11},{10,... | collective-permute-start | bytes 688136 | tf_op jit(solution)/shard_map/ppermute | solution.py:93
  207.6 16.6 %collective-permute-start.11 = (bf16[2,128,448]{1,2,0:T(8,128)(2,1)S(1)}, bf16[2,128,448]{1,2,0:T(8,128)(2,1)S(1)}, u32[]{:S(2)}, u32[]{:S(2)}) collective-permute-start(bf16[2,128,448]{1,2,0:T(8,128)(2,1)S(1)} %get-tuple-element.45), channel_id=1, source_target_pairs={{0,3},{1,2},{2,1},{3,0},{4,7},{5,6},{6,5},{7,4},{8,11},{9,10},{10,... | collective-permute-start | bytes 688136 | tf_op jit(solution)/shard_map/ppermute | solution.py:93
  210.7 20.2 %collective-permute-start.9 = (bf16[2,128,448]{1,2,0:T(8,128)(2,1)S(1)}, bf16[2,128,448]{1,2,0:T(8,128)(2,1)S(1)}, u32[]{:S(2)}, u32[]{:S(2)}) collective-permute-start(bf16[2,128,448]{1,2,0:T(8,128)(2,1)S(1)} %get-tuple-element.47), channel_id=1, source_target_pairs={{0,1},{1,0},{2,3},{3,2},{4,5},{5,4},{6,7},{7,6},{8,9},{9,8},{10,11... | collective-permute-start | bytes 688136 | tf_op jit(solution)/shard_map/ppermute | solution.py:93
  214.2 26.0 %collective-permute-start.8 = (bf16[128,448]{0,1:T(8,128)(2,1)S(1)}, bf16[128,448]{0,1:T(8,128)(2,1)S(1)}, u32[]{:S(2)}, u32[]{:S(2)}) collective-permute-start(bf16[128,448]{0,1:T(8,128)(2,1)S(1)} %dynamic-slice_bitcast_fusion.10), channel_id=1, source_target_pairs={{0,4},{4,0},{1,5},{5,1},{2,6},{6,2},{3,7},{7,3},{8,12},{12,8},{9,1... | collective-permute-start | bytes 344072 | tf_op jit(solution)/shard_map/ppermute | solution.py:14
  231.1 12.4 %collective-permute-start.12 = (bf16[128,448]{0,1:T(8,128)(2,1)S(1)}, bf16[128,448]{0,1:T(8,128)(2,1)S(1)}, u32[]{:S(2)}, u32[]{:S(2)}) collective-permute-start(bf16[128,448]{0,1:T(8,128)(2,1)S(1)} %get-tuple-element.48), channel_id=1, source_target_pairs={{0,23},{1,22},{2,21},{3,20},{4,19},{5,18},{6,17},{7,16},{16,7},{17... | collective-permute-start | bytes 344072 | tf_op jit(solution)/shard_map/ppermute | solution.py:18
  236.8 22.2 %collective-permute-start.13 = (bf16[128,448]{0,1:T(8,128)(2,1)S(1)}, bf16[128,448]{0,1:T(8,128)(2,1)S(1)}, u32[]{:S(2)}, u32[]{:S(2)}) collective-permute-start(bf16[128,448]{0,1:T(8,128)(2,1)S(1)} %get-tuple-element.49), channel_id=1, source_target_pairs={{0,19},{1,18},{2,17},{3,16},{4,23},{5,22},{6,21},{7,20},{16,3},{17... | collective-permute-start | bytes 344072 | tf_op jit(solution)/shard_map/ppermute | solution.py:163
